TPU v7x, 512 devices: a whole 4x4x16 slice. The times are simulated.
512 devices in a mesh: dp: 16 (over z), expert: 32 (over y, x, core).
Axes of the slice: x: 4, y: 4, z: 16, core: 2. Of those that a mesh axis runs over, the one named last changes fastest.
Arguments:
- tokens: bfloat16 [65536, 1024], P(('dp', 'expert')), may hold values from -6 to 6
- grad_out: bfloat16 [65536, 1024], P(('dp', 'expert')), may hold values from -6 to 6
- expert_ids: int32 [65536, 2], P(('dp', 'expert')), may hold values from 0 to 31, all different within a row; in each aligned block of 128 rows (0 to 127, 128 to 255, ...) at most 16 rows name the same one
- route_probs: bfloat16 [65536, 2], P(('dp', 'expert')), may hold values from 0.19921875 to 1
- gate_up_weight: bfloat16 [1024, 32, 1536], P('dp', 'expert'), may hold values from -0.1875 to 0.1875
- down_weight: bfloat16 [32, 768, 1024], P('expert'), may hold values from -0.21875 to 0.21875
- gate_up_scale_index: int32 [8, 32, 2], P(None, 'expert'), may hold values from 0 to 15
- down_scale_index: int32 [32, 6], P('expert'), may hold values from 0 to 15
- scale_table: float32 [16], replicated, may hold values from 0.5 to 2
Outputs:
- token_grad: bfloat16 [65536, 1024], P(('dp', 'expert'))
- prob_grad: float32 [65536, 2], P(('dp', 'expert'))
- gate_up_grad: bfloat16 [1024, 32, 1536], P('dp', 'expert')
- down_grad: bfloat16 [32, 768, 1024], P('expert')
Inputs may be any that keep to these rules, and one draw needn't show every extreme that they name: `expert_ids`: each row names two different experts. The 128 rows of one device name one expert at most 16 times, and in every draw some device's rows name some expert exactly 16 times.
All inputs are finite; a program needn't handle non-finite values.
Results may differ from a plain program's by a relative error of at most 0.022.
Values may be sent and summed in bfloat16 or wider, within the bound.
No kernel may reach another device: no remote copies, remote signals or barrier semaphores. Data moves between devices by JAX's collectives and lax.ppermute only.
A program may use at most 64 MiB of HBM per device.

v0:
```python
import jax
import jax.numpy as jnp
from jax import lax
from jax.sharding import PartitionSpec as P

QBLOCK = 128


def lookup(level_index, level_table):
    onehot = (level_index[..., None] == jnp.arange(level_table.shape[0], dtype=jnp.int32)).astype(
        level_table.dtype
    )
    return jnp.sum(onehot * level_table, axis=-1)


def slot_tables(routes, experts, capacity):
    flat_routes = routes.reshape(-1)
    expert_hits = (flat_routes[:, None] == jnp.arange(experts, dtype=jnp.int32)[None, :]).astype(
        jnp.int32
    )
    place = jnp.arange(flat_routes.shape[0], dtype=jnp.int32)
    earlier = (place[None, :] < place[:, None]).astype(jnp.bfloat16)
    before = jnp.dot(
        earlier, expert_hits.astype(jnp.bfloat16), preferred_element_type=jnp.float32
    ).astype(jnp.int32)
    slot_rank = jnp.sum(before * expert_hits, axis=1)
    destination = flat_routes * capacity + slot_rank
    table_hits = destination[:, None] == jnp.arange(experts * capacity, dtype=jnp.int32)[None, :]
    return table_hits.astype(jnp.float32).reshape(routes.shape[0], 2, experts * capacity)


def body(
    tokens,
    grad_out,
    expert_ids,
    route_probs,
    gate_up_weight,
    down_weight,
    gate_up_scale_index,
    down_scale_index,
    scale_table,
):
    high = lax.Precision.HIGHEST
    f32 = jnp.float32
    groups = lax.axis_size("expert")
    tok_dev = tokens.shape[0]
    model_width = tokens.shape[1]
    per_device = down_weight.shape[0]
    hidden = down_weight.shape[1]
    experts = per_device * groups
    capacity = 4 * tok_dev // experts
    slots_all = experts * capacity
    slot_hits = slot_tables(expert_ids, experts, capacity)
    either = (slot_hits[:, 0] + slot_hits[:, 1]).astype(jnp.bfloat16)
    row_shape = (groups, per_device, capacity, model_width)
    send_tokens = (
        jnp.einsum("ts,td->sd", either, tokens, preferred_element_type=f32)
        .astype(jnp.bfloat16)
        .reshape(row_shape)
    )
    send_grads = (
        jnp.einsum("ts,td->sd", either, grad_out, preferred_element_type=f32)
        .astype(jnp.bfloat16)
        .reshape(row_shape)
    )
    send_probs = (
        jnp.einsum("tks,tk->s", slot_hits, route_probs.astype(f32), precision=high)
        .astype(jnp.bfloat16)
        .reshape(row_shape[:3])
    )
    recv_tokens, recv_grads, recv_probs = (
        lax.all_to_all(send_tokens, "expert", split_axis=0, concat_axis=0, tiled=True),
        lax.all_to_all(send_grads, "expert", split_axis=0, concat_axis=0, tiled=True),
        lax.all_to_all(send_probs, "expert", split_axis=0, concat_axis=0, tiled=True),
    )
    level_rows = jnp.repeat(lookup(gate_up_scale_index, scale_table), QBLOCK, axis=0)
    full_scale = jnp.repeat(level_rows, hidden, axis=2)
    down_scale = jnp.repeat(lookup(down_scale_index, scale_table), QBLOCK, axis=1)
    down_eff = (down_weight.astype(f32) * down_scale[:, :, None]).astype(jnp.bfloat16)
    gathered = lax.all_gather(gate_up_weight, "dp", axis=0, tiled=True)
    gate_up_eff = (gathered.astype(f32) * full_scale).astype(jnp.bfloat16)
    projected = jnp.einsum("sjcd,djf->sjcf", recv_tokens, gate_up_eff, preferred_element_type=f32)
    gate_part = projected[..., :hidden]
    up_part = projected[..., hidden:]
    sigmoid_gate = jax.nn.sigmoid(gate_part)
    activated = gate_part * sigmoid_gate
    hidden_rows = (activated * up_part).astype(jnp.bfloat16)
    hidden_grad = jnp.einsum("sjcd,jfd->sjcf", recv_grads, down_eff, preferred_element_type=f32)
    probs_wide = recv_probs.astype(f32)[..., None]
    scaled_grad = probs_wide * hidden_grad
    gate_grad = scaled_grad * up_part * sigmoid_gate * (1.0 + gate_part * (1.0 - sigmoid_gate))
    up_grad = scaled_grad * activated
    joint_grad = jnp.concatenate([gate_grad, up_grad], axis=-1).astype(jnp.bfloat16)
    row_grads = jnp.einsum(
        "sjcf,djf->sjcd", joint_grad, gate_up_eff, preferred_element_type=f32
    ).astype(jnp.bfloat16)
    back_rows = lax.all_to_all(row_grads, "expert", split_axis=0, concat_axis=0, tiled=True)
    token_grad = jnp.dot(
        either, back_rows.reshape(slots_all, model_width), preferred_element_type=f32
    ).astype(jnp.bfloat16)
    expert_out = jnp.einsum("sjcf,jfd->sjcd", hidden_rows, down_eff, preferred_element_type=f32)
    back_out = lax.all_to_all(
        expert_out.astype(jnp.bfloat16), "expert", split_axis=0, concat_axis=0, tiled=True
    ).astype(expert_out.dtype)
    picked = jnp.einsum(
        "tks,sd->tkd", slot_hits, back_out.reshape(slots_all, model_width), precision=high
    )
    prob_grad = jnp.sum(picked * grad_out.astype(f32)[:, None, :], axis=-1)
    weighted = (probs_wide * hidden_rows.astype(f32)).astype(jnp.bfloat16)
    partial_sum = jnp.einsum("sjcd,sjcf->djf", recv_tokens, joint_grad, preferred_element_type=f32)
    gate_up_grad = lax.psum_scatter(
        (partial_sum * full_scale).astype(jnp.bfloat16), "dp", scatter_dimension=0, tiled=True
    )
    down_part = (
        jnp.einsum("sjcf,sjcd->jfd", weighted, recv_grads, preferred_element_type=f32)
        * down_scale[:, :, None]
    )
    down_grad = lax.psum(down_part.astype(jnp.bfloat16), "dp")
    return (token_grad, prob_grad, gate_up_grad, down_grad)


def solution(mesh):
    in_specs = (
        P(("dp", "expert"), None),
        P(("dp", "expert"), None),
        P(("dp", "expert"), None),
        P(("dp", "expert"), None),
        P("dp", "expert", None),
        P("expert", None, None),
        P(None, "expert", None),
        P("expert", None),
        P(),
    )
    out_specs = (
        P(("dp", "expert"), None),
        P(("dp", "expert"), None),
        P("dp", "expert", None),
        P("expert", None, None),
    )
    return jax.shard_map(body, mesh=mesh, in_specs=in_specs, out_specs=out_specs, check_vma=False)
```

profile of v0, /device:TPU:2, one launch (start us, length us, event | category | flops | bytes accessed | tf_op | source)
XLA Modules:
  0.0 353.9 jit_solution(2334480392853353179)
XLA Ops:
  11.6 9.4 %all-to-all-start = ((bf16[32,1,16]{2,1,0:T(2,128)(2,1)}), bf16[32,1,16]{2,1,0:T(2,128)(2,1)S(1)}, u32[]{:S(2)}, u32[]{:S(2)}) async-start(bf16[32,1,16]{2,1,0:T(2,128)(2,1)} %reshape.246), calls=%async_computation | async-start | bytes 32768 | tf_op jit(solution)/shard_map/all_to_all | solution.py:74
  21.2 1.4 convolution_convert_fusion.1
  22.6 4.5 %all-to-all-done = bf16[32,1,16]{2,1,0:T(2,128)(2,1)S(1)} async-done(((bf16[32,1,16]{2,1,0:T(2,128)(2,1)}), bf16[32,1,16]{2,1,0:T(2,128)(2,1)S(1)}, u32[]{:S(2)}, u32[]{:S(2)}) %all-to-all-start) | async-done | bytes 1056 | tf_op jit(solution)/shard_map/all_to_all | solution.py:74
  27.2 5.7 %all-to-all-start.2 = ((bf16[32,1,16,1024]{3,2,1,0:T(8,128)(2,1)}), bf16[32,1,16,1024]{3,2,1,0:T(8,128)(2,1)}, u32[]{:S(2)}, u32[]{:S(2)}) async-start(bf16[32,1,16,1024]{3,2,1,0:T(8,128)(2,1)} %bitcast.19), calls=%async_computation.2 | async-start | bytes 2097152 | tf_op jit(solution)/shard_map/all_to_all | solution.py:72
  34.0 1.5 convolution_convert_fusion.2
  35.5 55.5 %all-gather.2.cloned.1.call-done = bf16[1024,1,1536]{2,0,1:T(8,128)(2,1)} async-done(((bf16[64,1,1536]{2,0,1:T(8,128)(2,1)}), bf16[1024,1,1536]{2,0,1:T(8,128)(2,1)}) %all-gather.2.cloned.1.call-update) | async-done | bytes 3145744 | tf_op jit(solution)/shard_map/all_gather | solution.py:80
  91.0 3.2 copy.76
  94.2 7.2 %all-to-all-start.1 = ((bf16[32,1,16,1024]{3,2,1,0:T(8,128)(2,1)}), bf16[32,1,16,1024]{3,2,1,0:T(8,128)(2,1)}, u32[]{:S(2)}, u32[]{:S(2)}) async-start(bf16[32,1,16,1024]{3,2,1,0:T(8,128)(2,1)} %bitcast.139), calls=%async_computation.1 | async-start | bytes 2097152 | tf_op jit(solution)/shard_map/all_to_all | solution.py:73
  102.5 1.2 fusion.3
  103.7 1.7 copy-done.1
  105.4 1.7 copy-done.2
  107.1 5.1 %convolution_bitcast_fusion = f32[32,1,16,1536]{3,0,2,1:T(8,128)} fusion(bf16[1024,1536,1]{0,1,2:T(8,128)(2,1)S(1)} %fusion.3, bf16[32,1,16,1024]{3,2,1,0:T(8,128)(2,1)} %all-to-all-done.2), kind=kOutput, calls=%fused_computation.4 | convolution fusion | flops 1610612736 | bytes 7340032 | tf_op jit(solution)/shard_map/sjcd,djf->sjcf/dot_general | solution.py:82
  112.2 5.5 %all-to-all-done.1 = bf16[32,1,16,1024]{3,2,1,0:T(8,128)(2,1)} async-done(((bf16[32,1,16,1024]{3,2,1,0:T(8,128)(2,1)}), bf16[32,1,16,1024]{3,2,1,0:T(8,128)(2,1)}, u32[]{:S(2)}, u32[]{:S(2)}) %all-to-all-start.1) | async-done | bytes 1048608 | tf_op jit(solution)/shard_map/all_to_all | solution.py:73
  117.6 5.3 %fusion.31 = (bf16[32,16,768]{2,0,1:T(8,128)(2,1)S(1)}, bf16[32,16,768]{2,0,1:T(8,128)(2,1)S(1)}, bf16[32,1,16,768]{3,0,2,1:T(8,128)(2,1)}) fusion(f32[32,1,16,1536]{3,0,2,1:T(8,128)} %convolution_bitcast_fusion, bf16[32,1,16,1024]{3,2,1,0:T(8,128)(2,1)} %all-to-all-done.1, bf16[1,768,1024]{2,1,0:T(8,128)(2,1)S(1)} %copy-done.11, f32[768]{0:T(1024)S(1)} %copy-done.8, ...), kind=kOutput, calls=%fused_computation.49 | convolution fusion | flops 813957120 | bytes 8131584 | tf_op jit(solution)/shard_map/sjcd,jfd->sjcf/dot_general | solution.py:88
  123.0 3.8 %fusion.17 = f32[1536,1024,1]{1,0,2:T(8,128)S(1)} fusion(bf16[32,16,768]{2,0,1:T(8,128)(2,1)S(1)} %get-tuple-element.25, bf16[32,16,768]{2,0,1:T(8,128)(2,1)S(1)} %get-tuple-element.24, bf16[32,1,16,1024]{3,2,1,0:T(8,128)(2,1)} %all-to-all-done.2), kind=kOutput, calls=%fused_computation.36 | convolution fusion | flops 1613758464 | bytes 8912896 | tf_op jit(solution)/shard_map/sjcd,sjcf->djf/dot_general | solution.py:110
  126.8 1.8 fusion.2
  128.6 3.0 copy.96
  131.6 1.4 copy-done.12
  133.2 1.1 fusion.12
  134.3 1.6 copy.86
  135.8 5.7 %all-to-all-start.4 = ((bf16[32,1,16,1024]{3,2,1,0:T(8,128)(2,1)}), bf16[32,1,16,1024]{3,2,1,0:T(8,128)(2,1)}, u32[]{:S(2)}, u32[]{:S(2)}) async-start(bf16[32,1,16,1024]{3,2,1,0:T(8,128)(2,1)} %copy.86), calls=%async_computation.4 | async-start | bytes 2097152 | tf_op jit(solution)/shard_map/all_to_all | solution.py:102
  141.8 4.1 %fusion.11 = bf16[1,768,1024]{2,1,0:T(8,128)(2,1)} fusion(f32[768]{0:T(1024)S(1)} %copy-done.8, bf16[32,1,16,1024]{3,2,1,0:T(8,128)(2,1)} %all-to-all-done.1, bf16[32,1,16,768]{3,0,2,1:T(8,128)(2,1)} %get-tuple-element.26, f32[32,16]{0,1:T(8,128)S(1)} %copy.78), kind=kOutput, calls=%fused_computation.23 | convolution fusion | flops 808058880 | bytes 3412992 | tf_op jit(solution)/shard_map/sjcf,sjcd->jfd/dot_general | solution.py:115
  146.0 3.2 fusion.13
  149.2 1.6 copy.85
  150.7 7.1 %all-to-all-done.4 = bf16[32,1,16,1024]{3,2,1,0:T(8,128)(2,1)} async-done(((bf16[32,1,16,1024]{3,2,1,0:T(8,128)(2,1)}), bf16[32,1,16,1024]{3,2,1,0:T(8,128)(2,1)}, u32[]{:S(2)}, u32[]{:S(2)}) %all-to-all-start.4) | async-done | bytes 1048608 | tf_op jit(solution)/shard_map/all_to_all | solution.py:102
  157.8 5.0 %all-to-all-start.3 = ((bf16[32,1,16,1024]{3,2,1,0:T(8,128)(2,1)}), bf16[32,1,16,1024]{3,2,1,0:T(8,128)(2,1)S(1)}, u32[]{:S(2)}, u32[]{:S(2)}) async-start(bf16[32,1,16,1024]{3,2,1,0:T(8,128)(2,1)} %copy.85), calls=%async_computation.3 | async-start | bytes 2097152 | tf_op jit(solution)/shard_map/all_to_all | solution.py:97
  162.9 2.4 fusion.14
  165.3 13.8 %all-to-all-done.3 = bf16[32,1,16,1024]{3,2,1,0:T(8,128)(2,1)S(1)} async-done(((bf16[32,1,16,1024]{3,2,1,0:T(8,128)(2,1)}), bf16[32,1,16,1024]{3,2,1,0:T(8,128)(2,1)S(1)}, u32[]{:S(2)}, u32[]{:S(2)}) %all-to-all-start.3) | async-done | bytes 1048608 | tf_op jit(solution)/shard_map/all_to_all | solution.py:97
  180.1 22.4 %reduce-scatter.4.cloned.1.call-done = bf16[64,1536]{1,0:T(8,128)(2,1)} async-done(((bf16[1024,1536]{1,0:T(8,128)(2,1)}), bf16[64,1536]{1,0:T(8,128)(2,1)}) %reduce-scatter.4.cloned.1.call-update) | async-done | bytes 196624
  202.5 1.1 copy.97
  204.5 140.2 %all-reduce.2.cloned.1.call-done = bf16[1,768,1024]{2,1,0:T(8,128)(2,1)} async-done(((bf16[1,768,1024]{2,1,0:T(8,128)(2,1)}), bf16[1,768,1024]{2,1,0:T(8,128)(2,1)}) %all-reduce.2.cloned.1.call-update) | async-done | bytes 1572880 | tf_op jit(solution)/shard_map/psum | solution.py:118
  344.7 2.7 copy.122
  (65 shorter events, 9.2 us)
Async XLA Ops:
  7.2 14.0 %copy-start = (bf16[128,1024]{1,0:T(8,128)(2,1)S(1)}, bf16[128,1024]{1,0:T(8,128)(2,1)}, u32[]{:S(2)}) copy-start(bf16[128,1024]{1,0:T(8,128)(2,1)} %param.9) | copy-start | bytes 786436
  7.2 83.9 %all-gather.2.cloned.1.call-start = ((), (), s32[]{:S(2)}) async-start(), calls=%async_computation.6 | async-start | bytes 3342336 | tf_op jit(solution)/shard_map/all_gather | solution.py:80
  10.0 11.0 %copy-start.6 = (s32[128,2]{0,1:T(2,128)}, s32[128,2]{0,1:T(2,128)S(1)}, u32[]{:S(2)}) copy-start(s32[128,2]{0,1:T(2,128)S(1)} %multiply_add_fusion) | copy-start | bytes 3076
  11.6 15.6 %all-to-all-start = ((bf16[32,1,16]{2,1,0:T(2,128)(2,1)}), bf16[32,1,16]{2,1,0:T(2,128)(2,1)S(1)}, u32[]{:S(2)}, u32[]{:S(2)}) async-start(bf16[32,1,16]{2,1,0:T(2,128)(2,1)} %reshape.246), calls=%async_computation | async-start | bytes 32768 | tf_op jit(solution)/shard_map/all_to_all | solution.py:74
  21.1 11.8 %copy-start.9 = (s32[8,1,2]{0,2,1:T(2,128)S(1)}, s32[8,1,2]{0,2,1:T(2,128)}, u32[]{:S(2)}) copy-start(s32[8,1,2]{0,2,1:T(2,128)} %param.15) | copy-start | bytes 196
  21.1 11.8 %copy-start.10 = (f32[16]{0:T(128)S(1)}, f32[16]{0:T(128)}, u32[]{:S(2)}) copy-start(f32[16]{0:T(128)} %param.17) | copy-start | bytes 196
  21.1 12.0 %copy-start.13 = (s32[1,6]{1,0:T(1,128)S(1)}, s32[1,6]{1,0:T(1,128)}, u32[]{:S(2)}) copy-start(s32[1,6]{1,0:T(1,128)} %param.16) | copy-start | bytes 76
  21.2 12.9 %copy-start.4 = (bf16[128,1024]{1,0:T(8,128)(2,1)S(1)}, bf16[128,1024]{1,0:T(8,128)(2,1)}, u32[]{:S(2)}) copy-start(bf16[128,1024]{1,0:T(8,128)(2,1)} %param.10) | copy-start | bytes 786436
  27.2 67.1 %all-to-all-start.2 = ((bf16[32,1,16,1024]{3,2,1,0:T(8,128)(2,1)}), bf16[32,1,16,1024]{3,2,1,0:T(8,128)(2,1)}, u32[]{:S(2)}, u32[]{:S(2)}) async-start(bf16[32,1,16,1024]{3,2,1,0:T(8,128)(2,1)} %bitcast.19), calls=%async_computation.2 | async-start | bytes 2097152 | tf_op jit(solution)/shard_map/all_to_all | solution.py:72
  94.2 23.4 %all-to-all-start.1 = ((bf16[32,1,16,1024]{3,2,1,0:T(8,128)(2,1)}), bf16[32,1,16,1024]{3,2,1,0:T(8,128)(2,1)}, u32[]{:S(2)}, u32[]{:S(2)}) async-start(bf16[32,1,16,1024]{3,2,1,0:T(8,128)(2,1)} %bitcast.139), calls=%async_computation.1 | async-start | bytes 2097152 | tf_op jit(solution)/shard_map/all_to_all | solution.py:73
  101.5 101.0 %reduce-scatter.4.cloned.1.call-start = ((), (), s32[]{:S(2)}) async-start(), calls=%async_computation.8 | async-start | bytes 3342336
  102.5 2.9 copy-start.1
  105.3 1.7 copy-start.2
  107.1 10.6 %copy-start.8 = (f32[768]{0:T(1024)S(1)}, f32[768]{0:T(1024)}, u32[]{:S(2)}) copy-start(f32[768]{0:T(1024)} %broadcast_bitcast_fusion.1) | copy-start | bytes 9220
  107.1 10.6 %copy-start.11 = (bf16[1,768,1024]{2,1,0:T(8,128)(2,1)S(1)}, bf16[1,768,1024]{2,1,0:T(8,128)(2,1)}, u32[]{:S(2)}) copy-start(bf16[1,768,1024]{2,1,0:T(8,128)(2,1)} %param.14) | copy-start | bytes 4718596
  117.6 9.2 %slice-start = ((s8[6291456]{0:T(1024)(128)(4,1)}), s8[4194304]{0:T(1024)(128)(4,1)S(1)}, s32[]{:S(2)}) async-start(s8[6291456]{0:T(1024)(128)(4,1)} %bitcast.136), calls=%async_computation.9 | async-start | bytes 8388608
  122.9 3.8 %copy-start.15 = (bf16[32,16,768]{2,0,1:T(8,128)(2,1)}, bf16[32,16,768]{2,0,1:T(8,128)(2,1)S(1)}, u32[]{:S(2)}) copy-start(bf16[32,16,768]{2,0,1:T(8,128)(2,1)S(1)} %get-tuple-element.24) | copy-start | bytes 2359300
  122.9 3.8 %copy-start.16 = (bf16[32,16,768]{2,0,1:T(8,128)(2,1)}, bf16[32,16,768]{2,0,1:T(8,128)(2,1)S(1)}, u32[]{:S(2)}) copy-start(bf16[32,16,768]{2,0,1:T(8,128)(2,1)S(1)} %get-tuple-element.25) | copy-start | bytes 2359300
  123.0 3.9 %slice-start.1 = ((s8[6291456]{0:T(1024)(128)(4,1)}), s8[2097152]{0:T(1024)(128)(4,1)S(1)}, s32[]{:S(2)}) async-start(s8[6291456]{0:T(1024)(128)(4,1)} %bitcast.136), calls=%async_computation.10 | async-start | bytes 4194304
  131.6 1.4 copy-start.12
  131.6 1.6 copy-start.14
  135.8 22.0 %all-to-all-start.4 = ((bf16[32,1,16,1024]{3,2,1,0:T(8,128)(2,1)}), bf16[32,1,16,1024]{3,2,1,0:T(8,128)(2,1)}, u32[]{:S(2)}, u32[]{:S(2)}) async-start(bf16[32,1,16,1024]{3,2,1,0:T(8,128)(2,1)} %copy.86), calls=%async_computation.4 | async-start | bytes 2097152 | tf_op jit(solution)/shard_map/all_to_all | solution.py:102
  141.6 4.4 %copy-start.3 = (bf16[1024,1536,1]{0,1,2:T(8,128)(2,1)S(1)}, bf16[1024,1536,1]{0,1,2:T(8,128)(2,1)}, u32[]{:S(2)}) copy-start(bf16[1024,1536,1]{0,1,2:T(8,128)(2,1)} %copy-done.2) | copy-start | bytes 9437188
  141.6 203.2 %all-reduce.2.cloned.1.call-start = ((), (), s32[]{:S(2)}) async-start(), calls=%async_computation.7 | async-start | bytes 3145728 | tf_op jit(solution)/shard_map/psum | solution.py:118
  149.1 13.7 %copy-start.5 = (bf16[128,1024]{1,0:T(8,128)(2,1)S(1)}, bf16[128,1024]{1,0:T(8,128)(2,1)}, u32[]{:S(2)}) copy-start(bf16[128,1024]{1,0:T(8,128)(2,1)} %param.10) | copy-start | bytes 786436
  149.1 13.8 %copy-start.7 = (s32[128,2]{0,1:T(2,128)S(1)}, s32[128,2]{0,1:T(2,128)}, u32[]{:S(2)}) copy-start(s32[128,2]{0,1:T(2,128)} %copy-done.6) | copy-start | bytes 3076
  157.8 21.3 %all-to-all-start.3 = ((bf16[32,1,16,1024]{3,2,1,0:T(8,128)(2,1)}), bf16[32,1,16,1024]{3,2,1,0:T(8,128)(2,1)S(1)}, u32[]{:S(2)}, u32[]{:S(2)}) async-start(bf16[32,1,16,1024]{3,2,1,0:T(8,128)(2,1)} %copy.85), calls=%async_computation.3 | async-start | bytes 2097152 | tf_op jit(solution)/shard_map/all_to_all | solution.py:97
Sparse Core Ops, SparseCore 0:
  10.1 80.9 all-gather.1
  131.7 70.7 reduce-scatter.3
  205.4 139.2 all-reduce.1
where the time goes:
time: 355 us; the launch traced here: 354 us
  waiting for transfers between devices  250 us (70%)
  starting transfers between devices  33.6 us (9%)
  matrix products  29.9 us (8%)
  local copies, waits for them, and re-layouts  22.4 us (6%)
  between operations  14.1 us (4%)
  other arithmetic  4.22 us (1%)
    psum x1, waiting for transfers between devices, body(): down_grad = lax.psum(down_part.astype(jnp.bfloat16), 'dp')  140 us
    all_gather x1, waiting for transfers between devices, body(): gathered = lax.all_gather(gate_up_weight, 'dp', axis=0, tiled=True)  55.5 us
    unnamed x4, waiting for transfers between devices  23.1 us
    all_to_all x1, waiting for transfers between devices, body(): lax.all_to_all(row_grads, 'expert', split_axis=0, concat_axis=0, tiled=True)  13.8 us
    unnamed x45, local copies, waits for them, and re-layouts  13.5 us
    all_to_all x1, starting transfers between devices, body(): lax.all_to_all(send_probs, 'expert', split_axis=0, concat_axis=0, tiled=T...  9.4 us
    all_to_all x1, starting transfers between devices, body(): lax.all_to_all(send_grads, 'expert', split_axis=0, concat_axis=0, tiled=T...  7.21 us
    all_to_all x1, waiting for transfers between devices, body(): lax.all_to_all(expert_out.astype(jnp.bfloat16), 'expert', split_axis=0, c...  7.1 us
  transfers between devices with their start and end apart: 8, of which 7 were waited for; matrix products, arithmetic and copies ran while one was open for 10% of the time, Pallas kernels for 0%

commit v1 on v0

--- a/solution.py
+++ b/solution.py
@@ -77,7 +77,9 @@
     full_scale = jnp.repeat(level_rows, hidden, axis=2)
     down_scale = jnp.repeat(lookup(down_scale_index, scale_table), QBLOCK, axis=1)
     down_eff = (down_weight.astype(f32) * down_scale[:, :, None]).astype(jnp.bfloat16)
-    gathered = lax.all_gather(gate_up_weight, "dp", axis=0, tiled=True)
+    gathered = jnp.concatenate(
+        lax.all_to_all(jnp.stack([gate_up_weight] * lax.axis_size("dp")), "dp", 0, 0), axis=0
+    )
     gate_up_eff = (gathered.astype(f32) * full_scale).astype(jnp.bfloat16)
     projected = jnp.einsum("sjcd,djf->sjcf", recv_tokens, gate_up_eff, preferred_element_type=f32)
     gate_part = projected[..., :hidden]

time: 355 us -> 475 us (1.34)
  waiting for transfers between devices: 250 us -> 318 us
  local copies, waits for them, and re-layouts: 22.4 us -> 42.2 us
  blocking collectives: 0 us -> 14.8 us
  other arithmetic: 4.22 us -> 17.2 us
  starting transfers between devices: 33.6 us -> 38.4 us
    all_to_all x1, waiting for transfers between devices: 4.52 us -> 138 us  [body(): lax.all_to_all(jnp.stack([gate_up_weight] * lax.axis_size('dp')), 'dp', 0...]
    all_gather x1 -> x0, waiting for transfers between devices: 55.5 us -> none  [body(): gathered = lax.all_gather(gate_up_weight, 'dp', axis=0, tiled=True)]
    all_to_all x0 -> x1, blocking collectives: none -> 14.8 us  [body(): lax.all_to_all(send_probs, 'expert', split_axis=0, concat_axis=0, tiled=T...]
    convert_element_type x0 -> x2, local copies, waits for them, and re-layouts: none -> 13.4 us  [body(): gate_up_eff = (gathered.astype(f32) * full_scale).astype(jnp.bfloat16)]
    convert_element_type x0 -> x2, other arithmetic: none -> 11.3 us  [body(): gate_up_eff = (gathered.astype(f32) * full_scale).astype(jnp.bfloat16)]
    all_to_all x1, waiting for transfers between devices: 5.47 us -> 0.01 us  [body(): lax.all_to_all(send_grads, 'expert', split_axis=0, concat_axis=0, tiled=T...]
    unnamed x4 -> x3, waiting for transfers between devices: 23.1 us -> 19.8 us
    unnamed x45 -> x35, local copies, waits for them, and re-layouts: 13.5 us -> 15.2 us
  transfers between devices with their start and end apart: 8 -> 7, of which waited for: 7 -> 6; matrix products, arithmetic and copies ran while one was open for 10% -> 13% of each run, Pallas kernels for 0% -> 0%
where the time goes in v1:
time: 475 us; the launch traced here: 474 us
  waiting for transfers between devices  318 us (67%)
  local copies, waits for them, and re-layouts  42.2 us (9%)
  starting transfers between devices  38.4 us (8%)
  matrix products  29.3 us (6%)
  other arithmetic  17.2 us (4%)
  blocking collectives  14.8 us (3%)
  between operations  14.3 us (3%)
    psum x1, waiting for transfers between devices, body(): down_grad = lax.psum(down_part.astype(jnp.bfloat16), 'dp')  140 us
    all_to_all x1, waiting for transfers between devices, body(): lax.all_to_all(jnp.stack([gate_up_weight] * lax.axis_size('dp')), 'dp', 0...  138 us
    unnamed x3, waiting for transfers between devices  19.8 us
    unnamed x35, local copies, waits for them, and re-layouts  15.2 us
    all_to_all x1, blocking collectives, body(): lax.all_to_all(send_probs, 'expert', split_axis=0, concat_axis=0, tiled=T...  14.8 us
    all_to_all x1, starting transfers between devices, body(): lax.all_to_all(jnp.stack([gate_up_weight] * lax.axis_size('dp')), 'dp', 0...  14 us
    all_to_all x1, waiting for transfers between devices, body(): lax.all_to_all(row_grads, 'expert', split_axis=0, concat_axis=0, tiled=True)  13.7 us
    convert_element_type x2, local copies, waits for them, and re-layouts, body(): gate_up_eff = (gathered.astype(f32) * full_scale).astype(jnp.bfloat16)  13.4 us
  transfers between devices with their start and end apart: 7, of which 6 were waited for; matrix products, arithmetic and copies ran while one was open for 13% of the time, Pallas kernels for 0%

profile of v1, /device:TPU:2, one launch (start us, length us, event | category | flops | bytes accessed | tf_op | source)
XLA Modules:
  0.0 473.8 jit_solution(16496788401280869051)
XLA Ops:
  10.3 14.8 %all_to_all.30 = bf16[32,1,16]{2,1,0:T(2,128)(2,1)S(1)} all-to-all(bf16[32,1,16]{2,1,0:T(2,128)(2,1)S(1)} %reshape.285), channel_id=1, replica_groups=mesh['dp'=16,'expert'=32] {'expert'}, dimensions={0} | all-to-all | bytes 2048 | tf_op jit(solution)/shard_map/all_to_all | solution.py:74
  25.1 2.9 stack.2
  27.9 14.0 %all-to-all-start = ((bf16[16,64,1,1536]{3,1,2,0:T(8,128)(2,1)}), bf16[16,64,1,1536]{3,1,2,0:T(8,128)(2,1)S(1)}, u32[]{:S(2)}, u32[]{:S(2)}) async-start(bf16[16,64,1,1536]{3,1,2,0:T(8,128)(2,1)} %stack.2), calls=%async_computation | async-start | bytes 6291456 | tf_op jit(solution)/shard_map/all_to_all | solution.py:81
  43.5 137.8 %all-to-all-done = bf16[16,64,1,1536]{3,1,2,0:T(8,128)(2,1)S(1)} async-done(((bf16[16,64,1,1536]{3,1,2,0:T(8,128)(2,1)}), bf16[16,64,1,1536]{3,1,2,0:T(8,128)(2,1)S(1)}, u32[]{:S(2)}, u32[]{:S(2)}) %all-to-all-start) | async-done | bytes 3145760 | tf_op jit(solution)/shard_map/all_to_all | solution.py:81
  181.3 5.7 %all-to-all-start.3 = ((bf16[32,1,16,1024]{3,2,1,0:T(8,128)(2,1)}), bf16[32,1,16,1024]{3,2,1,0:T(8,128)(2,1)}, u32[]{:S(2)}, u32[]{:S(2)}) async-start(bf16[32,1,16,1024]{3,2,1,0:T(8,128)(2,1)} %bitcast.141), calls=%async_computation.3 | async-start | bytes 2097152 | tf_op jit(solution)/shard_map/all_to_all | solution.py:72
  189.8 1.5 broadcast_in_dim.14
  191.3 1.8 copy.88
  196.2 5.4 %reshape.276 = f32[1024,2,768]{2,1,0:T(2,128)} reshape(bf16[16,64,1,1536]{3,1,2,0:T(8,128)(2,1)S(1)} %all-to-all-done) | data formatting | bytes 9437184 | tf_op jit(solution)/shard_map/convert_element_type | solution.py:83
  201.7 1.6 all-to-all-done.3
  203.3 5.9 %all-to-all-start.2 = ((bf16[32,1,16,1024]{3,2,1,0:T(8,128)(2,1)}), bf16[32,1,16,1024]{3,2,1,0:T(8,128)(2,1)}, u32[]{:S(2)}, u32[]{:S(2)}) async-start(bf16[32,1,16,1024]{3,2,1,0:T(8,128)(2,1)} %bitcast.142), calls=%async_computation.2 | async-start | bytes 2097152 | tf_op jit(solution)/shard_map/all_to_all | solution.py:73
  209.4 7.3 %multiply_convert_fusion = bf16[1024,2,768]{2,1,0:T(2,128)(2,1)} fusion(f32[1024,2,768]{2,1,0:T(2,128)} %reshape.276, f32[1024,2]{1,0:T(8,128)} %bitcast.139), kind=kLoop, calls=%fused_computation.4 | loop fusion | flops 3145728 | bytes 9445376 | tf_op jit(solution)/shard_map/convert_element_type | solution.py:83
  216.7 8.0 %reshape.280 = bf16[1024,1536,1]{1,0,2:T(8,128)(2,1)} reshape(bf16[1024,2,768]{2,1,0:T(2,128)(2,1)} %multiply_convert_fusion) | data formatting | bytes 6291456 | tf_op jit(solution)/shard_map/convert_element_type | solution.py:83
  224.7 5.7 %convolution_bitcast_fusion = f32[32,1,16,1536]{3,0,2,1:T(8,128)} fusion(bf16[1024,1536,1]{1,0,2:T(8,128)(2,1)} %reshape.280, bf16[32,1,16,1024]{3,2,1,0:T(8,128)(2,1)} %all-to-all-done.3), kind=kOutput, calls=%fused_computation.5 | convolution fusion | flops 1610612736 | bytes 7340032 | tf_op jit(solution)/shard_map/sjcd,djf->sjcf/dot_general | solution.py:84
  230.4 5.6 %fusion.37 = (bf16[32,16,768]{2,0,1:T(8,128)(2,1)S(1)}, bf16[32,16,768]{2,0,1:T(8,128)(2,1)S(1)}, bf16[32,1,16,768]{3,0,2,1:T(8,128)(2,1)}) fusion(f32[32,1,16,1536]{3,0,2,1:T(8,128)} %convolution_bitcast_fusion, bf16[32,1,16,1024]{3,2,1,0:T(8,128)(2,1)} %all-to-all-done.2, bf16[1,768,1024]{2,1,0:T(8,128)(2,1)} %param.14, f32[768]{0:T(1024)S(1)} %copy-done.7, ...), kind=kOutput, calls=%fused_computation.51 | convolution fusion | flops 813957120 | bytes 8131584 | tf_op jit(solution)/shard_map/sjcd,jfd->sjcf/dot_general | solution.py:90
  236.1 3.8 fusion.23
  240.7 2.8 fusion.2
  243.5 4.7 %copy.86 = bf16[1024,1536]{1,0:T(8,128)(2,1)} copy(bf16[1024,1536]{0,1:T(8,128)(2,1)} %fusion.2) | data formatting | bytes 6291456
  248.2 2.7 broadcast_in_dim.32
  251.0 3.1 copy.89
  255.2 1.6 copy.79
  256.8 7.4 %all-to-all-start.5 = ((bf16[32,1,16,1024]{3,2,1,0:T(8,128)(2,1)}), bf16[32,1,16,1024]{3,2,1,0:T(8,128)(2,1)}, u32[]{:S(2)}, u32[]{:S(2)}) async-start(bf16[32,1,16,1024]{3,2,1,0:T(8,128)(2,1)} %copy.79), calls=%async_computation.5 | async-start | bytes 2097152 | tf_op jit(solution)/shard_map/all_to_all | solution.py:104
  264.3 3.8 fusion.15
  268.1 4.0 fusion.1
  272.1 1.8 fusion.17
  274.0 1.6 copy.78
  275.5 4.8 %all-to-all-done.5 = bf16[32,1,16,1024]{3,2,1,0:T(8,128)(2,1)} async-done(((bf16[32,1,16,1024]{3,2,1,0:T(8,128)(2,1)}), bf16[32,1,16,1024]{3,2,1,0:T(8,128)(2,1)}, u32[]{:S(2)}, u32[]{:S(2)}) %all-to-all-start.5) | async-done | bytes 1048608 | tf_op jit(solution)/shard_map/all_to_all | solution.py:104
  280.4 5.0 %all-to-all-start.4 = ((bf16[32,1,16,1024]{3,2,1,0:T(8,128)(2,1)}), bf16[32,1,16,1024]{3,2,1,0:T(8,128)(2,1)S(1)}, u32[]{:S(2)}, u32[]{:S(2)}) async-start(bf16[32,1,16,1024]{3,2,1,0:T(8,128)(2,1)} %copy.78), calls=%async_computation.4 | async-start | bytes 2097152 | tf_op jit(solution)/shard_map/all_to_all | solution.py:99
  285.5 2.4 fusion.20
  287.9 13.7 %all-to-all-done.4 = bf16[32,1,16,1024]{3,2,1,0:T(8,128)(2,1)S(1)} async-done(((bf16[32,1,16,1024]{3,2,1,0:T(8,128)(2,1)}), bf16[32,1,16,1024]{3,2,1,0:T(8,128)(2,1)S(1)}, u32[]{:S(2)}, u32[]{:S(2)}) %all-to-all-start.4) | async-done | bytes 1048608 | tf_op jit(solution)/shard_map/all_to_all | solution.py:99
  302.7 19.8 %reduce-scatter.4.cloned.1.call-done = bf16[64,1536]{1,0:T(8,128)(2,1)} async-done(((bf16[1024,1536]{1,0:T(8,128)(2,1)}), bf16[64,1536]{1,0:T(8,128)(2,1)}) %reduce-scatter.4.cloned.1.call-update) | async-done | bytes 196624
  324.4 139.9 %all-reduce.2.cloned.1.call-done = bf16[1,768,1024]{2,1,0:T(8,128)(2,1)} async-done(((bf16[1,768,1024]{2,1,0:T(8,128)(2,1)}), bf16[1,768,1024]{2,1,0:T(8,128)(2,1)}) %all-reduce.2.cloned.1.call-update) | async-done | bytes 1572880 | tf_op jit(solution)/shard_map/psum | solution.py:120
  464.3 2.7 copy.111
  (58 shorter events, 15.8 us)
Async XLA Ops:
  7.2 34.9 %copy-start = (bf16[128,1024]{1,0:T(8,128)(2,1)S(1)}, bf16[128,1024]{1,0:T(8,128)(2,1)}, u32[]{:S(2)}) copy-start(bf16[128,1024]{1,0:T(8,128)(2,1)} %param.9) | copy-start | bytes 786436
  9.3 32.6 %copy-start.5 = (s32[128,2]{0,1:T(2,128)}, s32[128,2]{0,1:T(2,128)S(1)}, u32[]{:S(2)}) copy-start(s32[128,2]{0,1:T(2,128)S(1)} %multiply_add_fusion) | copy-start | bytes 3076
  27.9 153.4 %all-to-all-start = ((bf16[16,64,1,1536]{3,1,2,0:T(8,128)(2,1)}), bf16[16,64,1,1536]{3,1,2,0:T(8,128)(2,1)S(1)}, u32[]{:S(2)}, u32[]{:S(2)}) async-start(bf16[16,64,1,1536]{3,1,2,0:T(8,128)(2,1)} %stack.2), calls=%async_computation | async-start | bytes 6291456 | tf_op jit(solution)/shard_map/all_to_all | solution.py:81
  43.5 151.2 %copy-start.2 = (bf16[128,1024]{1,0:T(8,128)(2,1)S(1)}, bf16[128,1024]{1,0:T(8,128)(2,1)}, u32[]{:S(2)}) copy-start(bf16[128,1024]{1,0:T(8,128)(2,1)} %param.10) | copy-start | bytes 786436
  181.3 22.0 %all-to-all-start.3 = ((bf16[32,1,16,1024]{3,2,1,0:T(8,128)(2,1)}), bf16[32,1,16,1024]{3,2,1,0:T(8,128)(2,1)}, u32[]{:S(2)}, u32[]{:S(2)}) async-start(bf16[32,1,16,1024]{3,2,1,0:T(8,128)(2,1)} %bitcast.141), calls=%async_computation.3 | async-start | bytes 2097152 | tf_op jit(solution)/shard_map/all_to_all | solution.py:72
  203.3 27.1 %all-to-all-start.2 = ((bf16[32,1,16,1024]{3,2,1,0:T(8,128)(2,1)}), bf16[32,1,16,1024]{3,2,1,0:T(8,128)(2,1)}, u32[]{:S(2)}, u32[]{:S(2)}) async-start(bf16[32,1,16,1024]{3,2,1,0:T(8,128)(2,1)} %bitcast.142), calls=%async_computation.2 | async-start | bytes 2097152 | tf_op jit(solution)/shard_map/all_to_all | solution.py:73
  209.2 113.2 %reduce-scatter.4.cloned.1.call-start = ((), (), s32[]{:S(2)}) async-start(), calls=%async_computation.8 | async-start | bytes 3342336
  224.7 5.7 %copy-start.7 = (f32[768]{0:T(1024)S(1)}, f32[768]{0:T(1024)}, u32[]{:S(2)}) copy-start(f32[768]{0:T(1024)} %broadcast_bitcast_fusion) | copy-start | bytes 9220
  236.1 3.8 copy-start.10
  236.1 3.8 copy-start.12
  236.1 3.8 copy-start.4
  251.0 3.1 copy-start.8
  251.0 3.1 copy-start.9
  256.8 23.6 %all-to-all-start.5 = ((bf16[32,1,16,1024]{3,2,1,0:T(8,128)(2,1)}), bf16[32,1,16,1024]{3,2,1,0:T(8,128)(2,1)}, u32[]{:S(2)}, u32[]{:S(2)}) async-start(bf16[32,1,16,1024]{3,2,1,0:T(8,128)(2,1)} %copy.79), calls=%async_computation.5 | async-start | bytes 2097152 | tf_op jit(solution)/shard_map/all_to_all | solution.py:104
  264.2 200.1 %all-reduce.2.cloned.1.call-start = ((), (), s32[]{:S(2)}) async-start(), calls=%async_computation.7 | async-start | bytes 3145728 | tf_op jit(solution)/shard_map/psum | solution.py:120
  268.1 4.0 copy-start.11
  268.1 4.0 copy-start.13
  274.0 11.5 %copy-start.3 = (bf16[128,1024]{1,0:T(8,128)(2,1)S(1)}, bf16[128,1024]{1,0:T(8,128)(2,1)}, u32[]{:S(2)}) copy-start(bf16[128,1024]{1,0:T(8,128)(2,1)} %param.10) | copy-start | bytes 786436
  274.0 11.5 %copy-start.6 = (s32[128,2]{0,1:T(2,128)S(1)}, s32[128,2]{0,1:T(2,128)}, u32[]{:S(2)}) copy-start(s32[128,2]{0,1:T(2,128)} %copy-done.5) | copy-start | bytes 3076
  280.4 21.3 %all-to-all-start.4 = ((bf16[32,1,16,1024]{3,2,1,0:T(8,128)(2,1)}), bf16[32,1,16,1024]{3,2,1,0:T(8,128)(2,1)S(1)}, u32[]{:S(2)}, u32[]{:S(2)}) async-start(bf16[32,1,16,1024]{3,2,1,0:T(8,128)(2,1)} %copy.78), calls=%async_computation.4 | async-start | bytes 2097152 | tf_op jit(solution)/shard_map/all_to_all | solution.py:99
  285.5 181.4 %copy-start.1 = (bf16[128,1024]{1,0:T(8,128)(2,1)S(1)}, bf16[128,1024]{1,0:T(8,128)(2,1)}, u32[]{:S(2)}) copy-start(bf16[128,1024]{1,0:T(8,128)(2,1)} %param.9) | copy-start | bytes 786436
Sparse Core Ops, SparseCore 0:
  248.4 74.0 reduce-scatter.3
  325.3 138.8 all-reduce.1
